TPU v7x, 32 devices: a whole 2x2x4 slice. The times are simulated.
32 devices in a mesh: band: 4 (over y, core), grid: 8 (over z, x).
Axes of the slice: x: 2, y: 2, z: 4, core: 2. Of those that a mesh axis runs over, the one named last changes fastest.
Arguments:
- ground: float32 [4, 128, 128, 128], P('band', 'grid'), may hold values from -6 to 6
- response: float32 [4, 2, 2, 128, 128, 128], P('band', None, None, None, 'grid'), may hold values from -0.6 to 0.6
- kernel_xc: float32 [128, 128, 128], P('grid'), may hold values from -2 to -0.3
Outputs:
- applied: float32 [4, 2, 2, 128, 128, 128], P('band', None, None, None, 'grid')
All inputs are finite; a program needn't handle non-finite values.
Results may differ from a plain program's by a relative error of at most 0.0001.
Values sent between devices are 32-bit elements; how exact they have to be, the bound alone decides.
A program may use at most 64 MiB of HBM per device.

v0:
```python
import math
import jax
import jax.numpy as jnp
from jax import lax
from jax.sharding import PartitionSpec as P

highest = lax.Precision.HIGHEST
spacing = 0.4527
einsum_forms = ("...xyz,xk->...kyz", "...xyz,yk->...xkz", "...xyz,zk->...xyk")


def dft_tables(length):
    positions = jnp.arange(length, dtype=jnp.int32)
    phases = positions[:, None] * positions[None, :] % length
    angles = phases.astype(jnp.float32) * (2.0 * math.pi / length)
    factor = 1.0 / math.sqrt(length)
    return (jnp.cos(angles) * factor, jnp.sin(angles) * factor)


def along(complex_pair, which_axis, tables, direction):
    real_part, imag_part = complex_pair
    cosine, sine_part = tables

    def contract(operand, matrix):
        return jnp.einsum(einsum_forms[which_axis], operand, matrix, precision=highest)

    new_real = contract(real_part, cosine) - direction * contract(imag_part, sine_part)
    new_imag = contract(imag_part, cosine) + direction * contract(real_part, sine_part)
    return (new_real, new_imag)


def signed_freq(positions, length):
    return jnp.where(positions < (length + 1) // 2, positions, positions - length).astype(
        jnp.float32
    )


def coulomb(freq_first, freq_second, freq_third, length):
    squares = (
        freq_first[:, None, None] ** 2
        + freq_second[None, :, None] ** 2
        + freq_third[None, None, :] ** 2
    )
    edge_len = spacing * length
    return jnp.where(
        squares > 0.5, edge_len * edge_len / (math.pi * jnp.maximum(squares, 1.0)), 0.0
    )


def scaled(complex_pair, weights):
    return (complex_pair[0] * weights, complex_pair[1] * weights)


def potential_whole(density, kernel_xc, tables, grid_len):
    wave_values = along(along(density, 1, tables, -1.0), 2, tables, -1.0)
    wave_values = (
        lax.all_to_all(wave_values[0], "grid", split_axis=1, concat_axis=0, tiled=True),
        lax.all_to_all(wave_values[1], "grid", split_axis=1, concat_axis=0, tiled=True),
    )
    wave_values = along(wave_values, 0, tables, -1.0)
    row_count = wave_values[0].shape[1]
    positions = jnp.arange(grid_len, dtype=jnp.int32)
    freq_second = signed_freq(
        lax.axis_index("grid") * row_count + jnp.arange(row_count, dtype=jnp.int32), grid_len
    )
    weights = coulomb(
        signed_freq(positions, grid_len), freq_second, signed_freq(positions, grid_len), grid_len
    )
    wave_values = along(scaled(wave_values, weights), 0, tables, 1.0)
    cell_values = (
        lax.all_to_all(wave_values[0], "grid", split_axis=0, concat_axis=1, tiled=True),
        lax.all_to_all(wave_values[1], "grid", split_axis=0, concat_axis=1, tiled=True),
    )
    cell_values = along(along(cell_values, 1, tables, 1.0), 2, tables, 1.0)
    return (cell_values[0] + kernel_xc * density[0], cell_values[1] + kernel_xc * density[1])


def on_device(ground, response, kernel_xc):
    grid_len = ground.shape[2]
    tables = dft_tables(grid_len)
    wave_values = (response[:, :, 0], response[:, :, 1])
    wave_values = along(along(wave_values, 0, tables, 1.0), 2, tables, 1.0)
    cell_values = (
        lax.all_to_all(wave_values[0], "grid", split_axis=2, concat_axis=3, tiled=True),
        lax.all_to_all(wave_values[1], "grid", split_axis=2, concat_axis=3, tiled=True),
    )
    cell_values = along(cell_values, 1, tables, 1.0)
    dens_real = jnp.sum(ground * (cell_values[0][:, 0] + cell_values[0][:, 1]), axis=0)
    dens_imag = jnp.sum(ground * (cell_values[1][:, 0] - cell_values[1][:, 1]), axis=0)
    density = lax.psum((dens_real, dens_imag), "band")
    pot_real, pot_imag = potential_whole(density, kernel_xc, tables, grid_len)
    prod_real = ground * pot_real
    prod_imag = ground * pot_imag
    fields = (jnp.stack((prod_real, prod_real), axis=1), jnp.stack((prod_imag, -prod_imag), axis=1))
    fields = along(along(fields, 1, tables, -1.0), 2, tables, -1.0)
    wave_out = (
        lax.all_to_all(fields[0], "grid", split_axis=3, concat_axis=2, tiled=True),
        lax.all_to_all(fields[1], "grid", split_axis=3, concat_axis=2, tiled=True),
    )
    wave_out = along(wave_out, 0, tables, -1.0)
    return jnp.stack(wave_out, axis=2)


def solution(mesh):
    return jax.shard_map(
        on_device,
        mesh=mesh,
        in_specs=(
            P("band", "grid", None, None),
            P("band", None, None, None, "grid", None),
            P("grid", None, None),
        ),
        out_specs=P("band", None, None, None, "grid", None),
        check_vma=False,
    )
```

profile of v0, /device:TPU:0, one launch (start us, length us, event | category | flops | bytes accessed | tf_op | source)
XLA Modules:
  0.0 492.5 jit_solution(3142891739396519265)
XLA Ops:
  11.7 2.6 fusion.19
  14.3 2.6 fusion.25
  16.9 2.6 fusion.24
  26.6 7.3 %all-to-all-start = ((f32[1,2,128,16,128]{4,3,1,0,2:T(8,128)}), f32[1,2,128,16,128]{4,3,1,0,2:T(8,128)}, u32[]{:S(2)}, u32[]{:S(2)}) async-start(f32[1,2,128,16,128]{4,3,1,0,2:T(8,128)} %copy.35), calls=%async_computation | async-start | bytes 4194304 | tf_op jit(solution)/shard_map/all_to_all | solution.py:84
  33.8 3.7 fusion.10
  42.2 40.0 %all-to-all-done = f32[1,2,128,16,128]{4,3,1,0,2:T(8,128)} async-done(((f32[1,2,128,16,128]{4,3,1,0,2:T(8,128)}), f32[1,2,128,16,128]{4,3,1,0,2:T(8,128)}, u32[]{:S(2)}, u32[]{:S(2)}) %all-to-all-start) | async-done | bytes 2097184 | tf_op jit(solution)/shard_map/all_to_all | solution.py:84
  82.2 4.4 all-to-all-start.1
  88.8 45.5 %all-to-all-done.1 = f32[1,2,128,16,128]{4,3,1,0,2:T(8,128)} async-done(((f32[1,2,128,16,128]{4,3,1,0,2:T(8,128)}), f32[1,2,128,16,128]{4,3,1,0,2:T(8,128)}, u32[]{:S(2)}, u32[]{:S(2)}) %all-to-all-start.1) | async-done | bytes 2097184 | tf_op jit(solution)/shard_map/all_to_all | solution.py:85
  146.8 50.8 %all-reduce.3.cloned.1.call-done = (f32[16,128,128]{2,1,0:T(8,128)}, f32[16,128,128]{2,1,0:T(8,128)}) async-done(((f32[16,128,128]{2,1,0:T(8,128)}, f32[16,128,128]{2,1,0:T(8,128)}), (f32[16,128,128]{2,1,0:T(8,128)}, f32[16,128,128]{2,1,0:T(8,128)})) %all-reduce.3.cloned.1.call-update) | async-done | bytes 2097168 | tf_op jit(solution)/shard_map/psum | solution.py:90
  208.4 5.5 %all-to-all-start.2 = ((f32[16,128,128]{2,0,1:T(8,128)}), f32[16,128,128]{2,0,1:T(8,128)}, u32[]{:S(2)}, u32[]{:S(2)}) async-start(f32[16,128,128]{2,0,1:T(8,128)} %copy.43), calls=%async_computation.2 | async-start | bytes 2097152 | tf_op jit(solution)/shard_map/all_to_all | solution.py:57
  218.0 21.8 %all-to-all-done.2 = f32[16,128,128]{2,0,1:T(8,128)} async-done(((f32[16,128,128]{2,0,1:T(8,128)}), f32[16,128,128]{2,0,1:T(8,128)}, u32[]{:S(2)}, u32[]{:S(2)}) %all-to-all-start.2) | async-done | bytes 1048608 | tf_op jit(solution)/shard_map/all_to_all | solution.py:57
  239.7 3.8 all-to-all-start.3
  245.0 24.5 %all-to-all-done.3 = f32[16,128,128]{2,0,1:T(8,128)S(1)} async-done(((f32[16,128,128]{2,0,1:T(8,128)}), f32[16,128,128]{2,0,1:T(8,128)S(1)}, u32[]{:S(2)}, u32[]{:S(2)}) %all-to-all-start.3) | async-done | bytes 1048608 | tf_op jit(solution)/shard_map/all_to_all | solution.py:58
  279.3 4.2 all-to-all-start.4
  287.7 21.5 %all-to-all-done.4 = f32[128,16,128]{2,1,0:T(8,128)} async-done(((f32[128,16,128]{2,1,0:T(8,128)}), f32[128,16,128]{2,1,0:T(8,128)}, u32[]{:S(2)}, u32[]{:S(2)}) %all-to-all-start.4) | async-done | bytes 1048608 | tf_op jit(solution)/shard_map/all_to_all | solution.py:71
  309.2 4.0 all-to-all-start.5
  314.5 24.0 %all-to-all-done.5 = f32[128,16,128]{2,1,0:T(8,128)S(1)} async-done(((f32[128,16,128]{2,1,0:T(8,128)}), f32[128,16,128]{2,1,0:T(8,128)S(1)}, u32[]{:S(2)}, u32[]{:S(2)}) %all-to-all-start.5) | async-done | bytes 1048608 | tf_op jit(solution)/shard_map/all_to_all | solution.py:72
  362.5 2.7 copy.59
  365.2 4.4 all-to-all-start.6
  369.6 3.7 fusion.2
  378.0 39.4 %all-to-all-done.6 = f32[1,2,16,128,128]{4,2,1,0,3:T(8,128)} async-done(((f32[1,2,16,128,128]{4,2,1,0,3:T(8,128)}), f32[1,2,16,128,128]{4,2,1,0,3:T(8,128)}, u32[]{:S(2)}, u32[]{:S(2)}) %all-to-all-start.6) | async-done | bytes 2097184 | tf_op jit(solution)/shard_map/all_to_all | solution.py:97
  417.4 4.4 all-to-all-start.7
  423.6 45.9 %all-to-all-done.7 = f32[1,2,16,128,128]{4,2,1,0,3:T(8,128)} async-done(((f32[1,2,16,128,128]{4,2,1,0,3:T(8,128)}), f32[1,2,16,128,128]{4,2,1,0,3:T(8,128)}, u32[]{:S(2)}, u32[]{:S(2)}) %all-to-all-start.7) | async-done | bytes 2097184 | tf_op jit(solution)/shard_map/all_to_all | solution.py:98
  480.8 4.4 copy.65
  (83 shorter events, 104.5 us)
Async XLA Ops:
  19.5 2.4 copy-start.1
  26.6 55.6 %all-to-all-start = ((f32[1,2,128,16,128]{4,3,1,0,2:T(8,128)}), f32[1,2,128,16,128]{4,3,1,0,2:T(8,128)}, u32[]{:S(2)}, u32[]{:S(2)}) async-start(f32[1,2,128,16,128]{4,3,1,0,2:T(8,128)} %copy.35), calls=%async_computation | async-start | bytes 4194304 | tf_op jit(solution)/shard_map/all_to_all | solution.py:84
  82.2 52.2 %all-to-all-start.1 = ((f32[1,2,128,16,128]{4,3,1,0,2:T(8,128)}), f32[1,2,128,16,128]{4,3,1,0,2:T(8,128)}, u32[]{:S(2)}, u32[]{:S(2)}) async-start(f32[1,2,128,16,128]{4,3,1,0,2:T(8,128)} %copy.39), calls=%async_computation.1 | async-start | bytes 4194304 | tf_op jit(solution)/shard_map/all_to_all | solution.py:85
  86.5 111.1 %all-reduce.3.cloned.1.call-start = ((), (), s32[]{:S(2)}) async-start(), calls=%async_computation.8 | async-start | bytes 4194304 | tf_op jit(solution)/shard_map/psum | solution.py:90
  142.7 2.3 copy-start.5
  197.6 2.6 copy-start.2
  201.5 2.7 copy-start.3
  208.4 31.3 %all-to-all-start.2 = ((f32[16,128,128]{2,0,1:T(8,128)}), f32[16,128,128]{2,0,1:T(8,128)}, u32[]{:S(2)}, u32[]{:S(2)}) async-start(f32[16,128,128]{2,0,1:T(8,128)} %copy.43), calls=%async_computation.2 | async-start | bytes 2097152 | tf_op jit(solution)/shard_map/all_to_all | solution.py:57
  239.7 29.7 %all-to-all-start.3 = ((f32[16,128,128]{2,0,1:T(8,128)}), f32[16,128,128]{2,0,1:T(8,128)S(1)}, u32[]{:S(2)}, u32[]{:S(2)}) async-start(f32[16,128,128]{2,0,1:T(8,128)} %copy.47), calls=%async_computation.3 | async-start | bytes 2097152 | tf_op jit(solution)/shard_map/all_to_all | solution.py:58
  279.3 29.9 %all-to-all-start.4 = ((f32[128,16,128]{2,1,0:T(8,128)}), f32[128,16,128]{2,1,0:T(8,128)}, u32[]{:S(2)}, u32[]{:S(2)}) async-start(f32[128,16,128]{2,1,0:T(8,128)} %copy.49), calls=%async_computation.4 | async-start | bytes 2097152 | tf_op jit(solution)/shard_map/all_to_all | solution.py:71
  309.2 29.4 %all-to-all-start.5 = ((f32[128,16,128]{2,1,0:T(8,128)}), f32[128,16,128]{2,1,0:T(8,128)S(1)}, u32[]{:S(2)}, u32[]{:S(2)}) async-start(f32[128,16,128]{2,1,0:T(8,128)} %copy.51), calls=%async_computation.5 | async-start | bytes 2097152 | tf_op jit(solution)/shard_map/all_to_all | solution.py:72
  343.8 2.5 copy-start.4
  343.9 2.5 copy-start.6
  343.9 2.5 copy-start.7
  358.2 2.2 copy-start
  365.2 52.2 %all-to-all-start.6 = ((f32[1,2,16,128,128]{4,2,1,0,3:T(8,128)}), f32[1,2,16,128,128]{4,2,1,0,3:T(8,128)}, u32[]{:S(2)}, u32[]{:S(2)}) async-start(f32[1,2,16,128,128]{4,2,1,0,3:T(8,128)} %copy.59), calls=%async_computation.6 | async-start | bytes 4194304 | tf_op jit(solution)/shard_map/all_to_all | solution.py:97
  417.4 52.2 %all-to-all-start.7 = ((f32[1,2,16,128,128]{4,2,1,0,3:T(8,128)}), f32[1,2,16,128,128]{4,2,1,0,3:T(8,128)}, u32[]{:S(2)}, u32[]{:S(2)}) async-start(f32[1,2,16,128,128]{4,2,1,0,3:T(8,128)} %copy.63), calls=%async_computation.7 | async-start | bytes 4194304 | tf_op jit(solution)/shard_map/all_to_all | solution.py:98
Sparse Core Ops, SparseCore 0:
  146.9 50.6 all-reduce.2
where the time goes:
time: 502 us; the launch traced here: 492 us
  waiting for transfers between devices  313 us (62%)
  matrix products  90.1 us (18%)
  starting transfers between devices  38.3 us (8%)
  local copies, waits for them, and re-layouts  33.9 us (7%)
  between operations  14.4 us (3%)
    dot_general x48, matrix products, contract(): jnp.einsum(einsum_forms[which_axis], operand, matrix, precision=highest)  90.1 us
    psum x1, waiting for transfers between devices, on_device(): density = lax.psum((dens_real, dens_imag), 'band')  50.8 us
    all_to_all x1, waiting for transfers between devices, on_device(): lax.all_to_all(fields[1], 'grid', split_axis=3, concat_axis=2, tiled=True)  45.9 us
    all_to_all x1, waiting for transfers between devices, on_device(): lax.all_to_all(wave_values[1], 'grid', split_axis=2, concat_axis=3, tiled...  45.5 us
    all_to_all x1, waiting for transfers between devices, on_device(): lax.all_to_all(wave_values[0], 'grid', split_axis=2, concat_axis=3, tiled...  40 us
    all_to_all x1, waiting for transfers between devices, on_device(): lax.all_to_all(fields[0], 'grid', split_axis=3, concat_axis=2, tiled=True)  39.4 us
    all_to_all x1, waiting for transfers between devices, potential_whole(): lax.all_to_all(wave_values[1], 'grid', split_axis=1, concat_axis=0, tiled...  24.5 us
    all_to_all x1, waiting for transfers between devices, potential_whole(): lax.all_to_all(wave_values[1], 'grid', split_axis=0, concat_axis=1, tiled...  24 us
  transfers between devices with their start and end apart: 9, of which 9 were waited for; matrix products, arithmetic and copies ran while one was open for 6% of the time, Pallas kernels for 0%

commit v1 on v0

--- a/solution.py
+++ b/solution.py
@@ -7,6 +7,28 @@
 highest = lax.Precision.HIGHEST
 spacing = 0.4527
 einsum_forms = ("...xyz,xk->...kyz", "...xyz,yk->...xkz", "...xyz,zk->...xyk")
+
+
+def split_up(x, dim, count):
+    before, after = (x.shape[:dim], x.shape[dim + 1 :])
+    return jnp.moveaxis(x.reshape(*before, count, -1, *after), dim, 0)
+
+
+def joined_along(blocks, dim):
+    blocks = jnp.moveaxis(blocks, 0, dim)
+    shape = blocks.shape
+    return blocks.reshape(*shape[:dim], shape[dim] * shape[dim + 1], *shape[dim + 2 :])
+
+
+def pairwise_exchange(value, axis, split_dim, concat_dim):
+    size, place = (lax.axis_size(axis), lax.axis_index(axis))
+    blocks = split_up(value, split_dim, size)
+    outs = [blocks[place]]
+    for hop in range(1, size):
+        sent = blocks[place ^ hop]
+        outs.append(lax.ppermute(sent, axis, [(i, i ^ hop) for i in range(size)]))
+    blocks = jnp.stack(outs)[place ^ jnp.arange(size)]
+    return joined_along(blocks, concat_dim)
 
 
 def dft_tables(length):
@@ -69,7 +91,7 @@
     wave_values = along(scaled(wave_values, weights), 0, tables, 1.0)
     cell_values = (
         lax.all_to_all(wave_values[0], "grid", split_axis=0, concat_axis=1, tiled=True),
-        lax.all_to_all(wave_values[1], "grid", split_axis=0, concat_axis=1, tiled=True),
+        pairwise_exchange(wave_values[1], "grid", 0, 1),
     )
     cell_values = along(along(cell_values, 1, tables, 1.0), 2, tables, 1.0)
     return (cell_values[0] + kernel_xc * density[0], cell_values[1] + kernel_xc * density[1])

time: 502 us -> 502 us (level)
  starting transfers between devices: 38.3 us -> 49.1 us
  waiting for transfers between devices: 313 us -> 303 us
    ppermute x0 -> x7, waiting for transfers between devices: none -> 34.5 us  [pairwise_exchange(): outs.append(lax.ppermute(sent, axis, [(i, i ^ hop) for i in range(size)]))]
    all_to_all x1 -> x0, waiting for transfers between devices: 24 us -> none  [potential_whole(): lax.all_to_all(wave_values[1], 'grid', split_axis=0, concat_axis=1, tiled...]
    all_to_all x1, waiting for transfers between devices: 21.5 us -> 0.01 us  [potential_whole(): lax.all_to_all(wave_values[0], 'grid', split_axis=0, concat_axis=1, tiled...]
    ppermute x0 -> x7, starting transfers between devices: none -> 14.1 us  [pairwise_exchange(): outs.append(lax.ppermute(sent, axis, [(i, i ^ hop) for i in range(size)]))]
  transfers between devices with their start and end apart: 9 -> 15, of which waited for: 9 -> 10; matrix products, arithmetic and copies ran while one was open for 6% -> 6% of each run, Pallas kernels for 0% -> 0%
where the time goes in v1:
time: 502 us; the launch traced here: 492 us
  waiting for transfers between devices  303 us (60%)
  matrix products  90 us (18%)
  starting transfers between devices  49.1 us (10%)
  local copies, waits for them, and re-layouts  33.5 us (7%)
  between operations  14.6 us (3%)
    dot_general x48, matrix products, contract(): jnp.einsum(einsum_forms[which_axis], operand, matrix, precision=highest)  90 us
    psum x1, waiting for transfers between devices, on_device(): density = lax.psum((dens_real, dens_imag), 'band')  50.8 us
    all_to_all x1, waiting for transfers between devices, on_device(): lax.all_to_all(fields[1], 'grid', split_axis=3, concat_axis=2, tiled=True)  45.9 us
    all_to_all x1, waiting for transfers between devices, on_device(): lax.all_to_all(wave_values[1], 'grid', split_axis=2, concat_axis=3, tiled...  45.5 us
    all_to_all x1, waiting for transfers between devices, on_device(): lax.all_to_all(wave_values[0], 'grid', split_axis=2, concat_axis=3, tiled...  40 us
    all_to_all x1, waiting for transfers between devices, on_device(): lax.all_to_all(fields[0], 'grid', split_axis=3, concat_axis=2, tiled=True)  39.8 us
    ppermute x7, waiting for transfers between devices, pairwise_exchange(): outs.append(lax.ppermute(sent, axis, [(i, i ^ hop) for i in range(size)]))  34.5 us
    all_to_all x1, waiting for transfers between devices, potential_whole(): lax.all_to_all(wave_values[1], 'grid', split_axis=1, concat_axis=0, tiled...  24.4 us
  transfers between devices with their start and end apart: 15, of which 10 were waited for; matrix products, arithmetic and copies ran while one was open for 6% of the time, Pallas kernels for 0%

profile of v1, /device:TPU:0, one launch (start us, length us, event | category | flops | bytes accessed | tf_op | source)
XLA Modules:
  0.0 492.4 jit_solution(8223370783388100206)
XLA Ops:
  14.3 2.6 fusion.25
  26.6 7.3 %all-to-all-start = ((f32[1,2,128,16,128]{4,3,1,0,2:T(8,128)}), f32[1,2,128,16,128]{4,3,1,0,2:T(8,128)}, u32[]{:S(2)}, u32[]{:S(2)}) async-start(f32[1,2,128,16,128]{4,3,1,0,2:T(8,128)} %copy.35), calls=%async_computation | async-start | bytes 4194304 | tf_op jit(solution)/shard_map/all_to_all | solution.py:106
  33.8 3.7 fusion.10
  42.2 40.0 %all-to-all-done = f32[1,2,128,16,128]{4,3,1,0,2:T(8,128)} async-done(((f32[1,2,128,16,128]{4,3,1,0,2:T(8,128)}), f32[1,2,128,16,128]{4,3,1,0,2:T(8,128)}, u32[]{:S(2)}, u32[]{:S(2)}) %all-to-all-start) | async-done | bytes 2097184 | tf_op jit(solution)/shard_map/all_to_all | solution.py:106
  82.2 4.4 all-to-all-start.1
  88.9 45.5 %all-to-all-done.1 = f32[1,2,128,16,128]{4,3,1,0,2:T(8,128)} async-done(((f32[1,2,128,16,128]{4,3,1,0,2:T(8,128)}), f32[1,2,128,16,128]{4,3,1,0,2:T(8,128)}, u32[]{:S(2)}, u32[]{:S(2)}) %all-to-all-start.1) | async-done | bytes 2097184 | tf_op jit(solution)/shard_map/all_to_all | solution.py:107
  146.9 50.8 %all-reduce.3.cloned.1.call-done = (f32[16,128,128]{2,1,0:T(8,128)}, f32[16,128,128]{2,1,0:T(8,128)}) async-done(((f32[16,128,128]{2,1,0:T(8,128)}, f32[16,128,128]{2,1,0:T(8,128)}), (f32[16,128,128]{2,1,0:T(8,128)}, f32[16,128,128]{2,1,0:T(8,128)})) %all-reduce.3.cloned.1.call-update) | async-done | bytes 2097168 | tf_op jit(solution)/shard_map/psum | solution.py:112
  208.5 5.5 %all-to-all-start.2 = ((f32[16,128,128]{2,0,1:T(8,128)}), f32[16,128,128]{2,0,1:T(8,128)}, u32[]{:S(2)}, u32[]{:S(2)}) async-start(f32[16,128,128]{2,0,1:T(8,128)} %copy.43), calls=%async_computation.2 | async-start | bytes 2097152 | tf_op jit(solution)/shard_map/all_to_all | solution.py:79
  218.0 21.7 %all-to-all-done.2 = f32[16,128,128]{2,0,1:T(8,128)} async-done(((f32[16,128,128]{2,0,1:T(8,128)}), f32[16,128,128]{2,0,1:T(8,128)}, u32[]{:S(2)}, u32[]{:S(2)}) %all-to-all-start.2) | async-done | bytes 1048608 | tf_op jit(solution)/shard_map/all_to_all | solution.py:79
  239.8 3.8 all-to-all-start.3
  245.1 24.4 %all-to-all-done.3 = f32[16,128,128]{2,0,1:T(8,128)S(1)} async-done(((f32[16,128,128]{2,0,1:T(8,128)}), f32[16,128,128]{2,0,1:T(8,128)S(1)}, u32[]{:S(2)}, u32[]{:S(2)}) %all-to-all-start.3) | async-done | bytes 1048608 | tf_op jit(solution)/shard_map/all_to_all | solution.py:80
  283.5 4.7 all-to-all-start.4
  288.2 4.7 collective-permute-start.6
  297.3 20.8 %collective-permute-done.1 = f32[16,16,128]{2,0,1:T(8,128)S(1)} collective-permute-done((f32[16,16,128]{2,0,1:T(8,128)S(1)}, f32[16,16,128]{2,0,1:T(8,128)S(1)}, u32[]{:S(2)}, u32[]{:S(2)}) %collective-permute-start.1) | collective-permute-done | bytes 131104 | tf_op jit(solution)/shard_map/ppermute | solution.py:29
  318.1 3.6 collective-permute-start.2
  321.7 4.5 collective-permute-done.2
  326.2 9.2 %collective-permute-done.3 = f32[16,16,128]{2,0,1:T(8,128)S(1)} collective-permute-done((f32[16,16,128]{2,0,1:T(8,128)S(1)}, f32[16,16,128]{2,0,1:T(8,128)S(1)}, u32[]{:S(2)}, u32[]{:S(2)}) %collective-permute-start.3) | collective-permute-done | bytes 131104 | tf_op jit(solution)/shard_map/ppermute | solution.py:29
  361.6 2.8 copy.58
  364.4 4.3 all-to-all-start.5
  368.7 3.7 fusion.2
  377.1 39.8 %all-to-all-done.5 = f32[1,2,16,128,128]{4,2,1,0,3:T(8,128)} async-done(((f32[1,2,16,128,128]{4,2,1,0,3:T(8,128)}), f32[1,2,16,128,128]{4,2,1,0,3:T(8,128)}, u32[]{:S(2)}, u32[]{:S(2)}) %all-to-all-start.5) | async-done | bytes 2097184 | tf_op jit(solution)/shard_map/all_to_all | solution.py:119
  416.9 4.6 all-to-all-start.6
  423.4 45.9 %all-to-all-done.6 = f32[1,2,16,128,128]{4,2,1,0,3:T(8,128)} async-done(((f32[1,2,16,128,128]{4,2,1,0,3:T(8,128)}), f32[1,2,16,128,128]{4,2,1,0,3:T(8,128)}, u32[]{:S(2)}, u32[]{:S(2)}) %all-to-all-start.6) | async-done | bytes 2097184 | tf_op jit(solution)/shard_map/all_to_all | solution.py:120
  480.6 4.4 copy.64
  (105 shorter events, 115.0 us)
Async XLA Ops:
  19.5 2.4 copy-start.1
  26.6 55.6 %all-to-all-start = ((f32[1,2,128,16,128]{4,3,1,0,2:T(8,128)}), f32[1,2,128,16,128]{4,3,1,0,2:T(8,128)}, u32[]{:S(2)}, u32[]{:S(2)}) async-start(f32[1,2,128,16,128]{4,3,1,0,2:T(8,128)} %copy.35), calls=%async_computation | async-start | bytes 4194304 | tf_op jit(solution)/shard_map/all_to_all | solution.py:106
  82.2 52.2 %all-to-all-start.1 = ((f32[1,2,128,16,128]{4,3,1,0,2:T(8,128)}), f32[1,2,128,16,128]{4,3,1,0,2:T(8,128)}, u32[]{:S(2)}, u32[]{:S(2)}) async-start(f32[1,2,128,16,128]{4,3,1,0,2:T(8,128)} %copy.39), calls=%async_computation.1 | async-start | bytes 4194304 | tf_op jit(solution)/shard_map/all_to_all | solution.py:107
  86.5 111.2 %all-reduce.3.cloned.1.call-start = ((), (), s32[]{:S(2)}) async-start(), calls=%async_computation.7 | async-start | bytes 4194304 | tf_op jit(solution)/shard_map/psum | solution.py:112
  142.7 2.3 copy-start.5
  197.7 2.6 copy-start.2
  201.6 2.7 copy-start.3
  208.5 31.3 %all-to-all-start.2 = ((f32[16,128,128]{2,0,1:T(8,128)}), f32[16,128,128]{2,0,1:T(8,128)}, u32[]{:S(2)}, u32[]{:S(2)}) async-start(f32[16,128,128]{2,0,1:T(8,128)} %copy.43), calls=%async_computation.2 | async-start | bytes 2097152 | tf_op jit(solution)/shard_map/all_to_all | solution.py:79
  239.8 29.7 %all-to-all-start.3 = ((f32[16,128,128]{2,0,1:T(8,128)}), f32[16,128,128]{2,0,1:T(8,128)S(1)}, u32[]{:S(2)}, u32[]{:S(2)}) async-start(f32[16,128,128]{2,0,1:T(8,128)} %copy.47), calls=%async_computation.3 | async-start | bytes 2097152 | tf_op jit(solution)/shard_map/all_to_all | solution.py:80
  279.2 16.7 %collective-permute-start = (f32[16,16,128]{2,0,1:T(8,128)S(1)}, f32[16,16,128]{2,0,1:T(8,128)S(1)}, u32[]{:S(2)}, u32[]{:S(2)}) collective-permute-start(f32[16,16,128]{2,0,1:T(8,128)S(1)} %get-tuple-element.15), channel_id=1, source_target_pairs={{0,1},{1,0},{2,3},{3,2},{4,5},{5,4},{6,7},{7,6},{8,9},{9,8},{10,11... | collective-permute-start | bytes 393224 | tf_op jit(solution)/shard_map/ppermute | solution.py:29
  283.5 54.2 %all-to-all-start.4 = ((f32[128,16,128]{2,1,0:T(8,128)}), f32[128,16,128]{2,1,0:T(8,128)}, u32[]{:S(2)}, u32[]{:S(2)}) async-start(f32[128,16,128]{2,1,0:T(8,128)} %copy.49), calls=%async_computation.4 | async-start | bytes 2097152 | tf_op jit(solution)/shard_map/all_to_all | solution.py:93
  288.2 47.3 %collective-permute-start.6 = (f32[16,16,128]{2,0,1:T(8,128)S(1)}, f32[16,16,128]{2,0,1:T(8,128)S(1)}, u32[]{:S(2)}, u32[]{:S(2)}) collective-permute-start(f32[16,16,128]{2,0,1:T(8,128)S(1)} %get-tuple-element.9), channel_id=1, source_target_pairs={{0,7},{1,6},{2,5},{3,4},{4,3},{5,2},{6,1},{7,0},{8,15},{9,14},{10,... | collective-permute-start | bytes 393224 | tf_op jit(solution)/shard_map/ppermute | solution.py:29
  292.9 42.6 %collective-permute-start.5 = (f32[16,16,128]{2,0,1:T(8,128)S(1)}, f32[16,16,128]{2,0,1:T(8,128)S(1)}, u32[]{:S(2)}, u32[]{:S(2)}) collective-permute-start(f32[16,16,128]{2,0,1:T(8,128)S(1)} %get-tuple-element.10), channel_id=1, source_target_pairs={{0,6},{1,7},{2,4},{3,5},{4,2},{5,3},{6,0},{7,1},{8,14},{9,15},{10,... | collective-permute-start | bytes 393224 | tf_op jit(solution)/shard_map/ppermute | solution.py:29
  293.4 42.0 %collective-permute-start.4 = (f32[16,16,128]{2,0,1:T(8,128)S(1)}, f32[16,16,128]{2,0,1:T(8,128)S(1)}, u32[]{:S(2)}, u32[]{:S(2)}) collective-permute-start(f32[16,16,128]{2,0,1:T(8,128)S(1)} %get-tuple-element.11), channel_id=1, source_target_pairs={{0,5},{1,4},{2,7},{3,6},{4,1},{5,0},{6,3},{7,2},{8,13},{9,12},{10,... | collective-permute-start | bytes 393224 | tf_op jit(solution)/shard_map/ppermute | solution.py:29
  294.0 41.4 %collective-permute-start.3 = (f32[16,16,128]{2,0,1:T(8,128)S(1)}, f32[16,16,128]{2,0,1:T(8,128)S(1)}, u32[]{:S(2)}, u32[]{:S(2)}) collective-permute-start(f32[16,16,128]{2,0,1:T(8,128)S(1)} %get-tuple-element.12), channel_id=1, source_target_pairs={{0,4},{1,5},{2,6},{3,7},{4,0},{5,1},{6,2},{7,3},{8,12},{9,13},{10,... | collective-permute-start | bytes 393224 | tf_op jit(solution)/shard_map/ppermute | solution.py:29
  295.9 22.2 %collective-permute-start.1 = (f32[16,16,128]{2,0,1:T(8,128)S(1)}, f32[16,16,128]{2,0,1:T(8,128)S(1)}, u32[]{:S(2)}, u32[]{:S(2)}) collective-permute-start(f32[16,16,128]{2,0,1:T(8,128)S(1)} %get-tuple-element.14), channel_id=1, source_target_pairs={{0,2},{1,3},{2,0},{3,1},{4,6},{5,7},{6,4},{7,5},{8,10},{9,11},{10,... | collective-permute-start | bytes 393224 | tf_op jit(solution)/shard_map/ppermute | solution.py:29
  318.1 8.1 %collective-permute-start.2 = (f32[16,16,128]{2,0,1:T(8,128)S(1)}, f32[16,16,128]{2,0,1:T(8,128)S(1)}, u32[]{:S(2)}, u32[]{:S(2)}) collective-permute-start(f32[16,16,128]{2,0,1:T(8,128)S(1)} %get-tuple-element.13), channel_id=1, source_target_pairs={{0,3},{1,2},{2,1},{3,0},{4,7},{5,6},{6,5},{7,4},{8,11},{9,10},{10,... | collective-permute-start | bytes 393224 | tf_op jit(solution)/shard_map/ppermute | solution.py:29
  343.0 2.5 copy-start.4
  343.0 2.5 copy-start.6
  343.0 2.5 copy-start.7
  357.3 2.2 copy-start
  364.4 52.6 %all-to-all-start.5 = ((f32[1,2,16,128,128]{4,2,1,0,3:T(8,128)}), f32[1,2,16,128,128]{4,2,1,0,3:T(8,128)}, u32[]{:S(2)}, u32[]{:S(2)}) async-start(f32[1,2,16,128,128]{4,2,1,0,3:T(8,128)} %copy.58), calls=%async_computation.5 | async-start | bytes 4194304 | tf_op jit(solution)/shard_map/all_to_all | solution.py:119
  416.9 52.4 %all-to-all-start.6 = ((f32[1,2,16,128,128]{4,2,1,0,3:T(8,128)}), f32[1,2,16,128,128]{4,2,1,0,3:T(8,128)}, u32[]{:S(2)}, u32[]{:S(2)}) async-start(f32[1,2,16,128,128]{4,2,1,0,3:T(8,128)} %copy.62), calls=%async_computation.6 | async-start | bytes 4194304 | tf_op jit(solution)/shard_map/all_to_all | solution.py:120
Sparse Core Ops, SparseCore 0:
  147.0 50.6 all-reduce.2
